TPU v7x, 32 devices: a whole 2x2x4 slice. The times are simulated.
32 devices in a mesh: grp: 4 (over y, x), seq: 4 (over z), mlp: 2 (over core).
Axes of the slice: x: 2, y: 2, z: 4, core: 2. Of those that a mesh axis runs over, the one named last changes fastest.
Arguments:
- queries: bfloat16 [16, 4, 4096], P('grp'), may hold values from -6 to 6
- new_keys: bfloat16 [16, 4, 4096], P(('grp', 'seq')), may hold values from -6 to 6
- new_values: bfloat16 [16, 4, 4096], P(('grp', 'seq')), may hold values from -6 to 6
- prefix_keys: bfloat16 [4, 2048, 4096], P('grp', ('seq', 'mlp')), may hold values from -250 to 250
- prefix_values: bfloat16 [4, 2048, 4096], P('grp', ('seq', 'mlp')), may hold values from -6 to 6
- tail_keys: bfloat16 [16, 256, 4096], P(('grp', 'seq'), 'mlp'), may hold values from -6 to 6
- tail_values: bfloat16 [16, 256, 4096], P(('grp', 'seq'), 'mlp'), may hold values from -6 to 6
- prefix_len: int32 [4], P('grp'), may hold values from 1 to 2048, as said below
- tail_len: int32 [16], P('grp'), may hold values from 0 to 256, as said below
- resid: bfloat16 [16, 4, 4096], P('grp', None, ('seq', 'mlp')), may hold values from -12 to 12
- w_out: bfloat16 [4096, 4096], P(None, ('seq', 'mlp')), may hold values from -0.09375 to 0.09375
- ln_gain: bfloat16 [4096], P(('seq', 'mlp')), may hold values from 0.25 to 1.75
- w_up: bfloat16 [4096, 16384], P(('seq', 'mlp'), 'grp'), may hold values from -0.09375 to 0.09375
- w_down: bfloat16 [16384, 4096], P('grp', ('seq', 'mlp')), may hold values from -0.046875 to 0.046875
Outputs:
- out: float32 [16, 4, 4096], P('grp', None, ('seq', 'mlp'))
Inputs may be any that keep to these rules, and one draw needn't show every extreme that they name: `prefix_len`: every group's live prefix is 1 to 2048 slots; in every draw some group's prefix fills all 2048 slots. `tail_len`: A request's live tail is 0 to 256 slots; in every draw some request's tail fills all 256 slots.
All inputs are finite; a program needn't handle non-finite values.
Results may differ from a plain program's by a relative error of at most 0.0075.
Values may be sent and summed in bfloat16 or wider, within the bound.
A program may use at most 128 MiB of HBM per device.

v0:
```python
import math
import jax
import jax.numpy as jnp
from jax import lax
from jax.sharding import PartitionSpec as P

D = 4096
H = 32
NEG = -1e30


def merged(value, axis, join):
    pieces = jax.tree.map(lambda part: lax.all_gather(part, axis), value)
    head = jax.tree.map(lambda part: part[0], pieces)
    tail = jax.tree.map(lambda part: part[1:], pieces)
    so_far, _ = lax.scan(lambda so_far, piece: (join(so_far, piece), None), head, tail)
    return so_far


def head_slopes(count):
    return jnp.power(2.0, -8.0 * (jnp.arange(count, dtype=jnp.float32) + 1.0) / count)


def attend(query_rows, key_block, value_block, query_pos, key_pos, key_mask):
    head_count = query_rows.shape[1]
    inv_scale = 1.0 / math.sqrt(query_rows.shape[2])
    scores = (
        jnp.einsum("qhd,khd->hqk", query_rows, key_block, preferred_element_type=jnp.float32)
        * inv_scale
    )
    distance = (query_pos[:, None] - key_pos[None, :]).astype(jnp.float32)
    scores = scores - head_slopes(head_count)[:, None, None] * distance[None, :, :]
    scores = jnp.where(key_mask, scores, NEG)
    row_max = jnp.max(scores, axis=2)
    weights = jnp.where(key_mask, jnp.exp(scores - row_max[:, :, None]), 0.0)
    weight_sum = jnp.sum(weights, axis=2)
    mixed_sum = jnp.einsum(
        "hqk,khd->qhd",
        weights.astype(jnp.bfloat16),
        value_block,
        preferred_element_type=jnp.float32,
    )
    return (row_max.T, weight_sum.T, mixed_sum)


def join_parts(first, second):
    best_max = jnp.maximum(first[0], second[0])
    factor_one = jnp.exp(first[0] - best_max)
    factor_two = jnp.exp(second[0] - best_max)
    return (
        best_max,
        first[1] * factor_one + second[1] * factor_two,
        first[2] * factor_one[:, :, None] + second[2] * factor_two[:, :, None],
    )


def body(
    queries,
    new_keys,
    new_values,
    prefix_keys,
    prefix_values,
    tail_keys,
    tail_values,
    prefix_len,
    tail_len,
    resid,
    w_out,
    ln_gain,
    w_up,
    w_down,
):
    group_req, step_count, model_width = queries.shape
    head_dim = model_width // H
    row_count = group_req * step_count
    seq_index = lax.axis_index("seq")
    core_index = lax.axis_index("mlp")
    block_len = prefix_keys.shape[1]
    tail_block = tail_keys.shape[1]
    block_start = (seq_index * lax.axis_size("mlp") + core_index) * block_len
    prefix_end = prefix_len[0]
    step_index = jnp.arange(step_count, dtype=jnp.int32)
    query_pos = prefix_end + jnp.repeat(tail_len, step_count) + jnp.tile(step_index, group_req)
    query_rows = queries.reshape(row_count, H, head_dim)
    key_pos = block_start + jnp.arange(block_len, dtype=jnp.int32)
    key_live = key_pos < prefix_end
    own_len = lax.dynamic_index_in_dim(tail_len, seq_index, 0, keepdims=False)
    own_rows = lax.dynamic_slice_in_dim(query_rows, seq_index * step_count, step_count, 0)
    own_pos = prefix_end + own_len + step_index
    tail_index = core_index * tail_block + jnp.arange(tail_block, dtype=jnp.int32)
    partial_value = attend(
        query_rows,
        prefix_keys[0].reshape(block_len, H, head_dim),
        prefix_values[0].reshape(block_len, H, head_dim),
        query_pos,
        key_pos,
        key_live[None, None, :],
    )
    tail_result = attend(
        own_rows,
        tail_keys[0].reshape(tail_block, H, head_dim),
        tail_values[0].reshape(tail_block, H, head_dim),
        own_pos,
        prefix_end + tail_index,
        (tail_index < own_len)[None, None, :],
    )
    self_mask = (step_index[None, :] <= step_index[:, None]) & (core_index == 0)
    self_result = attend(
        own_rows,
        new_keys[0].reshape(step_count, H, head_dim),
        new_values[0].reshape(step_count, H, head_dim),
        own_pos,
        own_pos,
        self_mask[None, :, :],
    )
    own_slice = tuple(
        (
            lax.dynamic_slice_in_dim(member, seq_index * step_count, step_count, 0)
            for member in partial_value
        )
    )
    own_part = join_parts(join_parts(own_slice, tail_result), self_result)
    partial_value = tuple(
        (
            lax.dynamic_update_slice_in_dim(member, update, seq_index * step_count, 0)
            for member, update in zip(partial_value, own_part)
        )
    )
    row_max, weight_sum, mixed_sum = merged(
        (partial_value[0], partial_value[1], partial_value[2]), ("seq", "mlp"), join_parts
    )
    attention = (
        (mixed_sum / weight_sum[:, :, None]).astype(jnp.bfloat16).reshape(row_count, model_width)
    )
    width_block = resid.shape[2]
    stream = resid.astype(jnp.float32).reshape(row_count, width_block) + jnp.dot(
        attention, w_out, preferred_element_type=jnp.float32
    )
    row_sums, squares = lax.psum(
        (jnp.sum(stream, axis=1), jnp.sum(stream * stream, axis=1)), ("seq", "mlp")
    )
    row_mean = row_sums / D
    row_var = squares / D - row_mean * row_mean
    hidden = (
        (stream - row_mean[:, None])
        * lax.rsqrt(row_var[:, None] + 1e-05)
        * ln_gain.astype(jnp.float32)
    ).astype(jnp.bfloat16)
    lifted = jnp.dot(
        lax.all_gather(hidden, "grp", axis=0, tiled=True), w_up, preferred_element_type=jnp.float32
    )
    summed = lax.psum(lifted, ("seq", "mlp"))
    activated = jax.nn.gelu(summed, approximate=False).astype(jnp.bfloat16)
    projected = lax.psum_scatter(
        jnp.dot(activated, w_down, preferred_element_type=jnp.float32),
        "grp",
        scatter_dimension=0,
        tiled=True,
    )
    return (stream + projected).reshape(group_req, step_count, width_block)


def solution(mesh):
    return jax.shard_map(
        body,
        mesh=mesh,
        in_specs=(
            P("grp", None, None),
            P(("grp", "seq"), None, None),
            P(("grp", "seq"), None, None),
            P("grp", ("seq", "mlp"), None),
            P("grp", ("seq", "mlp"), None),
            P(("grp", "seq"), "mlp", None),
            P(("grp", "seq"), "mlp", None),
            P("grp"),
            P("grp"),
            P("grp", None, ("seq", "mlp")),
            P(None, ("seq", "mlp")),
            P(("seq", "mlp")),
            P(("seq", "mlp"), "grp"),
            P("grp", ("seq", "mlp")),
        ),
        out_specs=P("grp", None, ("seq", "mlp")),
        check_vma=False,
    )
```

profile of v0, /device:TPU:0, one launch (start us, length us, event | category | flops | bytes accessed | tf_op | source)
XLA Modules:
  0.0 181.5 jit_solution(5606925134826433128)
XLA Ops:
  7.4 1.2 dynamic_slice.28
  9.2 0.6 fusion.102
  9.9 1.1 reshape.182
  11.0 1.4 copy.98
  12.5 0.7 fusion.143
  13.3 0.2 fusion.78
  13.8 0.5 copy.97
  14.4 1.2 fusion.142
  15.6 0.3 fusion.70
  16.1 0.2 fusion.81
  16.3 0.1 copy.72
  16.4 0.1 fusion.135
  16.5 0.1 fusion.88
  16.9 0.5 copy.99
  17.4 1.0 fusion.3
  18.4 0.2 copy-done.3
  18.6 0.2 copy.100
  18.9 0.1 copy.91
  18.9 0.1 copy.89
  19.1 0.5 fusion.22
  19.6 0.2 fusion.19
  19.8 0.8 copy.92
  20.7 0.1 copy.82
  20.8 0.2 dynamic_update_slice.13
  21.0 15.8 %all_gather.32 = f32[8,16,32]{2,1,0:T(8,128)S(1)} all-gather(f32[1,16,32]{2,1,0:T(8,128)S(1)} %copy.83), channel_id=1, replica_groups=mesh['grp'=4,'seq'=4,'mlp'=2] {'seq','mlp'}, dimensions={0}, use_global_device_ids=true | all-gather | bytes 18432 | tf_op jit(solution)/shard_map/all_gather | solution.py:13
  37.0 0.2 dynamic_update_slice.12
  37.2 14.1 %all_gather.29 = f32[8,16,32]{2,1,0:T(8,128)S(1)} all-gather(f32[1,16,32]{2,1,0:T(8,128)S(1)} %copy.76), channel_id=1, replica_groups=mesh['grp'=4,'seq'=4,'mlp'=2] {'seq','mlp'}, dimensions={0}, use_global_device_ids=true | all-gather | bytes 18432 | tf_op jit(solution)/shard_map/all_gather | solution.py:13
  51.4 1.7 all-gather.2.cloned.1.call-done
  53.1 1.7 slice.29
  54.8 1.0 slice_bitcast_fusion
  55.8 2.2 %while.14 = (s32[]{:T(128)}, f32[16,32]{1,0:T(8,128)S(1)}, f32[16,32]{1,0:T(8,128)S(1)}, f32[16,32,128]{2,1,0:T(8,128)S(1)}, f32[7,16,32]{2,1,0:T(8,128)S(1)}, /...) while((s32[]{:T(128)}, f32[16,32]{1,0:T(8,128)S(1)}, f32[16,32]{1,0:T(8,128)S(1)}, ...), condition=%wide.region_7.8_spmd, body=%wide.region_6.7_spmd.sunk | while | flops 199682 | bytes 807005 | solution.py:16
  55.8 0.3 fusion.153
  56.1 0.3 fusion.153
  56.4 0.3 fusion.153
  56.8 0.3 fusion.153
  57.1 0.3 fusion.153
  57.4 0.3 fusion.153
  57.7 0.3 fusion.153
  58.0 0.1 divide_convert_fusion
  58.1 3.0 %fusion.137 = (f32[16]{0:T(128)S(1)}, f32[16]{0:T(128)S(1)}, f32[16,512]{1,0:T(8,128)S(1)}) fusion(f32[16,512]{1,0:T(8,128)S(1)} %reshape.186, bf16[4096,512]{1,0:T(8,128)(2,1)} %param.26, bf16[2,8,32,128]{3,2,1,0:T(8,128)(2,1)S(1)} %bitcast.177), kind=kOutput, calls=%fused_computation.181 | convolution fusion | flops 67141600 | bytes 4391040 | tf_op jit(solution)/shard_map/dot_general | solution.py:136
  61.1 15.5 %all-reduce = (f32[16]{0:T(128)S(1)}, f32[16]{0:T(128)S(1)}) all-reduce(f32[16]{0:T(128)S(1)} %get-tuple-element.60, f32[16]{0:T(128)S(1)} %get-tuple-element.59), channel_id=1, replica_groups=mesh['grp'=4,'seq'=4,'mlp'=2] {'seq','mlp'}, use_global_device_ids=true, to_apply=%region_11.12 | all-reduce | flops 32 | bytes 256 | tf_op jit(solution)/shard_map/psum | solution.py:139
  76.6 8.1 %all_gather.36 = bf16[64,512]{1,0:T(8,128)(2,1)S(1)} all-gather(bf16[16,512]{1,0:T(8,128)(2,1)S(1)} %multiply_convert_fusion), channel_id=1, replica_groups=mesh['grp'=4,'seq'=4,'mlp'=2] {'grp'}, dimensions={0}, use_global_device_ids=true | all-gather | bytes 81920 | tf_op jit(solution)/shard_map/all_gather | solution.py:150
  84.8 4.1 %fusion.144 = f32[64,4096]{1,0:T(8,128)} fusion(bf16[64,512]{1,0:T(8,128)(2,1)S(1)} %all_gather.36, bf16[512,4096]{1,0:T(8,128)(2,1)} %param.28), kind=kOutput, calls=%fused_computation.184 | convolution fusion | flops 268435456 | bytes 5308416 | tf_op jit(solution)/shard_map/dot_general | solution.py:149
  88.9 56.1 %all-reduce.3.cloned.1.call-done = f32[64,4096]{1,0:T(8,128)} async-done(((f32[64,4096]{1,0:T(8,128)}), f32[64,4096]{1,0:T(8,128)}) %all-reduce.3.cloned.1.call-update) | async-done | bytes 1048592 | tf_op jit(solution)/shard_map/psum | solution.py:152
  145.1 5.5 %fusion.37 = f32[64,512]{1,0:T(8,128)} fusion(bf16[4096,512]{1,0:T(8,128)(2,1)} %param.29, f32[64,4096]{1,0:T(8,128)} %all-reduce.3.cloned.1.call-done), kind=kOutput, calls=%fused_computation.49 | convolution fusion | flops 285474816 | bytes 5373952 | tf_op jit(solution)/shard_map/dot_general | solution.py:155
  150.6 22.9 %reduce-scatter.2.cloned.1.call-done = f32[16,512]{1,0:T(8,128)} async-done(((f32[64,512]{1,0:T(8,128)}), f32[16,512]{1,0:T(8,128)}) %reduce-scatter.2.cloned.1.call-update) | async-done | bytes 32784 | tf_op jit(solution)/shard_map/reduce_scatter | solution.py:154
  173.6 0.8 add.168
  174.3 0.6 reshape.184
  (61 shorter events, 1.8 us)
Async XLA Ops:
  6.5 13.1 %copy-start = (bf16[1,4,4096]{2,1,0:T(4,128)(2,1)S(1)}, bf16[1,4,4096]{2,1,0:T(4,128)(2,1)}, u32[]{:S(2)}) copy-start(bf16[1,4,4096]{2,1,0:T(4,128)(2,1)} %param.18) | copy-start | bytes 98308
  6.5 7.1 %copy-start.7 = (s32[4]{0:T(128)S(1)}, s32[4]{0:T(128)}, u32[]{:S(2)}) copy-start(s32[4]{0:T(128)} %param.24) | copy-start | bytes 52
  6.5 7.2 %copy-start.1 = (bf16[1,256,4096]{2,1,0:T(8,128)(2,1)S(1)}, bf16[1,256,4096]{2,1,0:T(8,128)(2,1)}, u32[]{:S(2)}) copy-start(bf16[1,256,4096]{2,1,0:T(8,128)(2,1)} %param.19) | copy-start | bytes 6291460
  6.5 46.6 %all-gather.2.cloned.1.call-start = ((), (), s32[]{:S(2)}) async-start(), calls=%async_computation.1 | async-start | bytes 2359296 | tf_op jit(solution)/shard_map/all_gather | solution.py:13
  14.3 1.8 copy-start.4
  14.3 2.6 %copy-start.2 = (bf16[1,256,4096]{2,1,0:T(8,128)(2,1)S(1)}, bf16[1,256,4096]{2,1,0:T(8,128)(2,1)}, u32[]{:S(2)}) copy-start(bf16[1,256,4096]{2,1,0:T(8,128)(2,1)} %param.20) | copy-start | bytes 6291460
  17.3 1.2 copy-start.3
  18.8 32.5 %copy-start.5 = (bf16[4,4,512]{2,1,0:T(4,128)(2,1)S(1)}, bf16[4,4,512]{2,1,0:T(4,128)(2,1)}, u32[]{:S(2)}) copy-start(bf16[4,4,512]{2,1,0:T(4,128)(2,1)} %param.25) | copy-start | bytes 49156
  18.8 32.5 %copy-start.6 = (bf16[512]{0:T(512)(128)(2,1)S(1)}, bf16[512]{0:T(512)(128)(2,1)}, u32[]{:S(2)}) copy-start(bf16[512]{0:T(512)(128)(2,1)} %param.27) | copy-start | bytes 3076
  20.6 124.4 %all-reduce.3.cloned.1.call-start = ((), (), s32[]{:S(2)}) async-start(), calls=%async_computation.2 | async-start | bytes 2097152 | tf_op jit(solution)/shard_map/psum | solution.py:152
  88.9 84.7 %reduce-scatter.2.cloned.1.call-start = ((), (), s32[]{:S(2)}) async-start(), calls=%async_computation.3 | async-start | bytes 163840 | tf_op jit(solution)/shard_map/reduce_scatter | solution.py:154
Sparse Core Ops, SparseCore 0:
  20.8 32.3 all-gather.1
  89.0 56.0 all-reduce.2
  150.7 22.7 reduce-scatter.1
where the time goes:
time: 182 us; the launch traced here: 181 us
  waiting for transfers between devices  80.9 us (44%)
  blocking collectives  53.5 us (29%)
  matrix products  16.5 us (9%)
  between operations  14.8 us (8%)
  local copies, waits for them, and re-layouts  11 us (6%)
  other arithmetic  4.55 us (2%)
    psum x1, waiting for transfers between devices, body(): summed = lax.psum(lifted, ('seq', 'mlp'))  56.1 us
    all_gather x2, blocking collectives, merged(): pieces = jax.tree.map(lambda part: lax.all_gather(part, axis), value)  29.9 us
    reduce_scatter x1, waiting for transfers between devices, body(): lax.psum_scatter(jnp.dot(activated, w_down, preferred_element_type=jnp.fl...  22.9 us
    psum x1, blocking collectives, body(): lax.psum((jnp.sum(stream, axis=1), jnp.sum(stream * stream, axis=1)), ('s...  15.5 us
    all_gather x1, blocking collectives, body(): lax.all_gather(hidden, 'grp', axis=0, tiled=True)  8.13 us
    dot_general x1, matrix products, body(): jnp.dot(activated, w_down, preferred_element_type=jnp.float32)  5.52 us
    dot_general x1, matrix products, body(): jnp.dot(lax.all_gather(hidden, 'grp', axis=0, tiled=True), w_up, preferre...  4.1 us
  transfers between devices with their start and end apart: 3, of which 3 were waited for; matrix products, arithmetic and copies ran while one was open for 0% of the time, Pallas kernels for 0%

commit v1 on v0

--- a/solution.py
+++ b/solution.py
@@ -149,7 +149,8 @@
     lifted = jnp.dot(
         lax.all_gather(hidden, "grp", axis=0, tiled=True), w_up, preferred_element_type=jnp.float32
     )
-    summed = lax.psum(lifted, ("seq", "mlp"))
+    step_out = lax.all_gather(lifted, axis_name=("seq", "mlp"))
+    summed = jnp.sum(step_out, 0)
     activated = jax.nn.gelu(summed, approximate=False).astype(jnp.bfloat16)
     projected = lax.psum_scatter(
         jnp.dot(activated, w_down, preferred_element_type=jnp.float32),

time: 182 us -> 215 us (1.18)
  waiting for transfers between devices: 80.9 us -> 104 us
  other arithmetic: 4.55 us -> 12.7 us
    all_gather x0 -> x1, waiting for transfers between devices: none -> 79.4 us  [body(): step_out = lax.all_gather(lifted, axis_name=('seq', 'mlp'))]
    psum x1 -> x0, waiting for transfers between devices: 56.1 us -> none  [body(): summed = lax.psum(lifted, ('seq', 'mlp'))]
    reduce_sum x0 -> x1, other arithmetic: none -> 3.97 us  [body(): summed = jnp.sum(step_out, 0)]
where the time goes in v1:
time: 215 us; the launch traced here: 214 us
  waiting for transfers between devices  104 us (48%)
  blocking collectives  53.6 us (25%)
  matrix products  17.2 us (8%)
  between operations  14.8 us (7%)
  other arithmetic  12.7 us (6%)
  local copies, waits for them, and re-layouts  11.8 us (5%)
    all_gather x1, waiting for transfers between devices, body(): step_out = lax.all_gather(lifted, axis_name=('seq', 'mlp'))  79.4 us
    all_gather x2, blocking collectives, merged(): pieces = jax.tree.map(lambda part: lax.all_gather(part, axis), value)  30.1 us
    reduce_scatter x1, waiting for transfers between devices, body(): lax.psum_scatter(jnp.dot(activated, w_down, preferred_element_type=jnp.fl...  22.5 us
    psum x1, blocking collectives, body(): lax.psum((jnp.sum(stream, axis=1), jnp.sum(stream * stream, axis=1)), ('s...  15.4 us
    all_gather x1, blocking collectives, body(): lax.all_gather(hidden, 'grp', axis=0, tiled=True)  8.13 us
    dot_general x1, matrix products, body(): jnp.dot(activated, w_down, preferred_element_type=jnp.float32)  4.77 us
  transfers between devices with their start and end apart: 3, of which 3 were waited for; matrix products, arithmetic and copies ran while one was open for 0% of the time, Pallas kernels for 0%

profile of v1, /device:TPU:0, one launch (start us, length us, event | category | flops | bytes accessed | tf_op | source)
XLA Modules:
  0.0 214.0 jit_solution(2038052570618687835)
XLA Ops:
  7.2 1.3 dynamic_slice.28
  9.3 1.2 fusion.102
  10.5 0.6 iota_add_fusion.1
  11.1 0.5 broadcast_compare_fusion
  11.6 0.7 broadcast_add_fusion
  12.3 0.6 add.150
  13.0 0.7 subtract_convert_fusion.2
  13.7 1.1 reshape.182
  14.9 0.9 fusion.81
  16.0 0.7 fusion.88
  16.9 1.4 copy.98
  18.3 1.5 fusion.143
  19.9 0.8 fusion.78
  20.8 1.2 copy.100
  22.1 0.5 copy.97
  22.8 1.2 fusion.142
  24.0 0.3 fusion.70
  24.9 0.5 copy.99
  25.4 1.0 fusion.3
  26.6 0.5 fusion.22
  27.1 0.2 fusion.19
  27.3 0.8 copy.92
  28.3 0.2 dynamic_update_slice.13
  28.7 15.8 %all_gather.38 = f32[8,16,32]{2,1,0:T(8,128)S(1)} all-gather(f32[1,16,32]{2,1,0:T(8,128)S(1)} %copy.83), channel_id=1, replica_groups=mesh['grp'=4,'seq'=4,'mlp'=2] {'seq','mlp'}, dimensions={0}, use_global_device_ids=true | all-gather | bytes 18432 | tf_op jit(solution)/shard_map/all_gather | solution.py:13
  44.5 0.2 dynamic_update_slice.12
  44.8 14.2 %all_gather.35 = f32[8,16,32]{2,1,0:T(8,128)S(1)} all-gather(f32[1,16,32]{2,1,0:T(8,128)S(1)} %copy.76), channel_id=1, replica_groups=mesh['grp'=4,'seq'=4,'mlp'=2] {'seq','mlp'}, dimensions={0}, use_global_device_ids=true | all-gather | bytes 18432 | tf_op jit(solution)/shard_map/all_gather | solution.py:13
  59.0 1.7 all-gather.4.cloned.1.call-done
  60.7 1.1 slice_bitcast_fusion
  61.8 0.5 slice-done
  62.3 2.1 while.14
  62.3 0.3 fusion.153
  62.6 0.3 fusion.153
  62.9 0.3 fusion.153
  63.2 0.3 fusion.153
  63.5 0.3 fusion.153
  63.8 0.3 fusion.153
  64.1 0.3 fusion.153
  64.4 0.1 divide_convert_fusion
  64.6 3.0 %fusion.137 = (f32[16]{0:T(128)S(1)}, f32[16]{0:T(128)S(1)}, f32[16,512]{1,0:T(8,128)S(1)}) fusion(f32[16,512]{1,0:T(8,128)S(1)} %reshape.186, bf16[4096,512]{1,0:T(8,128)(2,1)} %param.26, bf16[2,8,32,128]{3,2,1,0:T(8,128)(2,1)S(1)} %bitcast.179), kind=kOutput, calls=%fused_computation.181 | convolution fusion | flops 67141600 | bytes 4391040 | tf_op jit(solution)/shard_map/dot_general | solution.py:136
  67.5 15.4 %all-reduce = (f32[16]{0:T(128)S(1)}, f32[16]{0:T(128)S(1)}) all-reduce(f32[16]{0:T(128)S(1)} %get-tuple-element.60, f32[16]{0:T(128)S(1)} %get-tuple-element.59), channel_id=1, replica_groups=mesh['grp'=4,'seq'=4,'mlp'=2] {'seq','mlp'}, use_global_device_ids=true, to_apply=%region_11.12 | all-reduce | flops 32 | bytes 256 | tf_op jit(solution)/shard_map/psum | solution.py:139
  83.0 8.1 %all_gather.42 = bf16[64,512]{1,0:T(8,128)(2,1)S(1)} all-gather(bf16[16,512]{1,0:T(8,128)(2,1)S(1)} %multiply_convert_fusion), channel_id=1, replica_groups=mesh['grp'=4,'seq'=4,'mlp'=2] {'grp'}, dimensions={0}, use_global_device_ids=true | all-gather | bytes 81920 | tf_op jit(solution)/shard_map/all_gather | solution.py:150
  91.1 4.1 %fusion.144 = f32[64,4096]{1,0:T(8,128)} fusion(bf16[64,512]{1,0:T(8,128)(2,1)S(1)} %all_gather.42, bf16[512,4096]{1,0:T(8,128)(2,1)} %param.28), kind=kOutput, calls=%fused_computation.184 | convolution fusion | flops 268435456 | bytes 5308416 | tf_op jit(solution)/shard_map/dot_general | solution.py:149
  95.3 79.4 %all-gather.6.cloned.1.call-done = f32[512,4096]{1,0:T(8,128)} async-done(((f32[64,4096]{1,0:T(8,128)}), f32[512,4096]{1,0:T(8,128)}) %all-gather.6.cloned.1.call-update) | async-done | bytes 8388624 | tf_op jit(solution)/shard_map/all_gather | solution.py:152
  174.7 4.0 %reduce_sum.59 = f32[64,4096]{1,0:T(8,128)S(1)} reduce(f32[8,64,4096]{2,1,0:T(8,128)} %bitcast.169, f32[]{:T(128)} %constant.25.clone.1), dimensions={0}, to_apply=%region_12.13 | reduce | flops 1835008 | bytes 9437188 | tf_op jit(solution)/shard_map/reduce_sum | solution.py:153
  178.7 4.8 %fusion.37 = f32[64,512]{1,0:T(8,128)} fusion(bf16[4096,512]{1,0:T(8,128)(2,1)} %param.29, f32[64,4096]{1,0:T(8,128)S(1)} %reduce_sum.59), kind=kOutput, calls=%fused_computation.49 | convolution fusion | flops 285474816 | bytes 5373952 | tf_op jit(solution)/shard_map/dot_general | solution.py:156
  183.5 22.5 %reduce-scatter.2.cloned.1.call-done = f32[16,512]{1,0:T(8,128)} async-done(((f32[64,512]{1,0:T(8,128)}), f32[16,512]{1,0:T(8,128)}) %reduce-scatter.2.cloned.1.call-update) | async-done | bytes 32784 | tf_op jit(solution)/shard_map/reduce_scatter | solution.py:155
  206.0 0.8 add.166
  206.8 0.6 reshape.184
  (83 shorter events, 2.4 us)
Async XLA Ops:
  6.5 20.6 %copy-start = (bf16[1,4,4096]{2,1,0:T(4,128)(2,1)S(1)}, bf16[1,4,4096]{2,1,0:T(4,128)(2,1)}, u32[]{:S(2)}) copy-start(bf16[1,4,4096]{2,1,0:T(4,128)(2,1)} %param.18) | copy-start | bytes 98308
  6.5 54.2 %all-gather.4.cloned.1.call-start = ((), (), s32[]{:S(2)}) async-start(), calls=%async_computation.1 | async-start | bytes 2359296 | tf_op jit(solution)/shard_map/all_gather | solution.py:13
  6.5 10.3 %copy-start.12 = (f32[32]{0:T(128)}, f32[32]{0:T(128)S(1)}, u32[]{:S(2)}) copy-start(f32[32]{0:T(128)S(1)} %multiply_power_fusion) | copy-start | bytes 388
  13.7 7.2 %copy-start.3 = (bf16[1,128,4096]{2,1,0:T(8,128)(2,1)S(1)}, bf16[1,128,4096]{2,1,0:T(8,128)(2,1)}, u32[]{:S(2)}) copy-start(bf16[1,128,4096]{2,1,0:T(8,128)(2,1)} %param.22) | copy-start | bytes 3145732
  16.0 0.8 copy-start.5
  16.8 1.5 copy-start.11
  16.8 1.5 copy-start.16
  18.3 3.7 %copy-start.1 = (bf16[1,256,4096]{2,1,0:T(8,128)(2,1)S(1)}, bf16[1,256,4096]{2,1,0:T(8,128)(2,1)}, u32[]{:S(2)}) copy-start(bf16[1,256,4096]{2,1,0:T(8,128)(2,1)} %param.19) | copy-start | bytes 6291460
  22.0 0.6 copy-start.10
  22.0 0.7 copy-start.15
  22.0 0.7 copy-start.9
  22.0 0.7 copy-start.13
  22.7 1.8 copy-start.6
  22.7 1.8 copy-start.8
  22.7 2.2 %copy-start.2 = (bf16[1,256,4096]{2,1,0:T(8,128)(2,1)S(1)}, bf16[1,256,4096]{2,1,0:T(8,128)(2,1)}, u32[]{:S(2)}) copy-start(bf16[1,256,4096]{2,1,0:T(8,128)(2,1)} %param.20) | copy-start | bytes 6291460
  25.4 1.2 copy-start.4
  25.4 1.2 copy-start.17
  25.4 2.8 %copy-start.14 = (bf16[512]{0:T(512)(128)(2,1)S(1)}, bf16[512]{0:T(512)(128)(2,1)}, u32[]{:S(2)}) copy-start(bf16[512]{0:T(512)(128)(2,1)} %param.27) | copy-start | bytes 3076
  25.4 2.8 %copy-start.7 = (bf16[4,4,512]{2,1,0:T(4,128)(2,1)S(1)}, bf16[4,4,512]{2,1,0:T(4,128)(2,1)}, u32[]{:S(2)}) copy-start(bf16[4,4,512]{2,1,0:T(4,128)(2,1)} %param.25) | copy-start | bytes 49156
  28.1 146.6 %all-gather.6.cloned.1.call-start = ((), (), s32[]{:S(2)}) async-start(), calls=%async_computation.3 | async-start | bytes 9437184 | tf_op jit(solution)/shard_map/all_gather | solution.py:152
  60.7 1.6 slice-start
  95.3 110.7 %reduce-scatter.2.cloned.1.call-start = ((), (), s32[]{:S(2)}) async-start(), calls=%async_computation.2 | async-start | bytes 163840 | tf_op jit(solution)/shard_map/reduce_scatter | solution.py:155
Sparse Core Ops, SparseCore 0:
  28.3 32.3 all-gather.3
  95.4 79.2 all-gather.5
  183.6 22.3 reduce-scatter.1
